TPU v7x, 768 devices: a whole 4x8x12 slice. The times are simulated.
768 devices in a mesh: blk: 384 (over z, y, x_hi, core), inner: 2 (over x_lo).
Axes of the slice: x: 4 (x_hi: 2, x_lo: 2; x = x_hi * 2 + x_lo), y: 8, z: 12, core: 2. Of those that a mesh axis runs over, the one named last changes fastest.
Arguments:
- picture_vectors: bfloat16 [294912, 1152], P(('blk', 'inner')), may hold values from -0.29882812 to 0.29882812
- caption_vectors: bfloat16 [294912, 1152], P(('blk', 'inner')), may hold values from -0.29882812 to 0.29882812
- score_scaling: float32 [], replicated, may hold values from 5 to 20
- score_shift: float32 [], replicated, may hold values from -3 to 0
Outputs:
- loss_rows: float32 [294912], P(('blk', 'inner'))
- image_grad: bfloat16 [294912, 1152], P(('blk', 'inner'))
- text_grad: bfloat16 [294912, 1152], P(('blk', 'inner'))
All inputs are finite; a program needn't handle non-finite values.
Results may differ from a plain program's by a relative error of at most 0.0061.
Values may be sent and summed in bfloat16 or wider, within the bound.
A program may use at most 32 MiB of HBM per device.

v0:
```python
import jax
import jax.numpy as jnp
from jax import lax
from jax.sharding import PartitionSpec as P

SPAN = 4


def from_behind(value, axis, steps):
    count = lax.axis_size(axis)
    pairs = [(source, (source + steps) % count) for source in range(count)]
    return lax.ppermute(value, axis, pairs)


def normalize(block):
    values = block.astype(jnp.float32)
    length = jnp.sqrt(jnp.sum(values * values, axis=-1, keepdims=True) + 1e-06)
    return (values / length, length)


def matrix_entries(
    picture_summed, caption_summed, score_scaling, score_shift, first_round_indicator
):
    match_scores = (
        score_scaling
        * lax.dot_general(
            picture_summed,
            caption_summed,
            (((1,), (1,)), ((), ())),
            preferred_element_type=jnp.float32,
        )
        + score_shift
    )
    rows = match_scores.shape[0]
    if first_round_indicator:
        same = jnp.arange(rows)[:, None] == jnp.arange(rows)[None, :]
        match_sign = jnp.where(same, jnp.float32(1.0), jnp.float32(-1.0))
    else:
        match_sign = jnp.float32(-1.0)
    objective_total = jnp.sum(jax.nn.softplus(-match_sign * match_scores), axis=1)
    score_multiplier = (
        -match_sign * jax.nn.sigmoid(-match_sign * match_scores) * score_scaling
    ).astype(jnp.bfloat16)
    return (objective_total, score_multiplier)


def project(unit, grad, length):
    return (grad - unit * jnp.sum(unit * grad, axis=-1, keepdims=True)) / length


def back_term(score_multiplier, picture_summed):
    return lax.dot_general(
        score_multiplier,
        picture_summed,
        (((0,), (0,)), ((), ())),
        preferred_element_type=jnp.float32,
    )


def local(picture_vectors, caption_vectors, score_scaling, score_shift):
    rows = picture_vectors.shape[0]
    image_unit, image_length = normalize(picture_vectors)
    text_unit, text_length = normalize(caption_vectors)
    picture_summed = image_unit.astype(jnp.bfloat16)
    caption_summed = text_unit.astype(jnp.bfloat16)
    loss_total = jnp.zeros((rows,), jnp.float32)
    grad_image = jnp.zeros(picture_vectors.shape, jnp.float32)
    current_tile = caption_summed
    running = jnp.zeros(picture_vectors.shape, jnp.float32)
    for peer_distance in range(SPAN):
        if peer_distance > 0:
            current_tile = from_behind(current_tile, ("blk", "inner"), 1)
        objective_total, score_multiplier = matrix_entries(
            picture_summed, current_tile, score_scaling, score_shift, peer_distance == 0
        )
        loss_total = loss_total + objective_total
        grad_image = grad_image + jnp.dot(
            score_multiplier, current_tile, preferred_element_type=jnp.float32
        )
        term = back_term(score_multiplier, picture_summed)
        if peer_distance == 0:
            running = term
        else:
            running = from_behind(running, ("blk", "inner"), 1) + term
    grad_text = from_behind(running, ("blk", "inner"), 1 - SPAN)
    loss_rows = loss_total / (SPAN * rows)
    image_grad = project(image_unit, grad_image, image_length).astype(jnp.bfloat16)
    text_grad = project(text_unit, grad_text, text_length).astype(jnp.bfloat16)
    return (loss_rows, image_grad, text_grad)


def solution(mesh):
    in_specs = (P(("blk", "inner"), None), P(("blk", "inner"), None), P(), P())
    out_specs = (P(("blk", "inner")), P(("blk", "inner"), None), P(("blk", "inner"), None))
    return jax.shard_map(local, mesh=mesh, in_specs=in_specs, out_specs=out_specs, check_vma=False)
```

profile of v0, /device:TPU:1, one launch (start us, length us, event | category | flops | bytes accessed | tf_op | source)
XLA Modules:
  0.0 247.4 jit_solution(3763448383955289146)
XLA Ops:
  0.6 0.0 copy-start
  1.4 1.4 fusion
  2.8 1.4 fusion.11
  4.2 0.0 copy-done
  4.3 0.3 fusion.1
  4.5 0.3 fusion.12
  5.4 1.0 fusion.7
  6.5 0.7 fusion.15
  7.1 3.9 %collective-permute-start.3 = (f32[384,1152]{1,0:T(8,128)S(1)}, f32[384,1152]{1,0:T(8,128)S(1)}, u32[]{:S(2)}, u32[]{:S(2)}) collective-permute-start(f32[384,1152]{1,0:T(8,128)S(1)} %fusion.15), channel_id=1, source_target_pairs={{0,1},{1,2},{2,3},{3,4},{4,5},{5,6},{6,7},{7,8},{8,9},{9,10},{10,1... | collective-permute-start | bytes 5308424 | tf_op jit(solution)/shard_map/ppermute | solution.py:12
  11.1 3.7 %collective-permute-start = (bf16[384,1152]{1,0:T(8,128)(2,1)S(1)}, bf16[384,1152]{1,0:T(8,128)(2,1)S(1)}, u32[]{:S(2)}, u32[]{:S(2)}) collective-permute-start(bf16[384,1152]{1,0:T(8,128)(2,1)S(1)} %fusion.12), channel_id=1, source_target_pairs={{0,1},{1,2},{2,3},{3,4},{4,5},{5,6},{6,7},{7,8},{8,9},{9,10},{10,1... | collective-permute-start | bytes 2654216 | tf_op jit(solution)/shard_map/ppermute | solution.py:12
  14.8 44.9 %collective-permute-done = bf16[384,1152]{1,0:T(8,128)(2,1)S(1)} collective-permute-done((bf16[384,1152]{1,0:T(8,128)(2,1)S(1)}, bf16[384,1152]{1,0:T(8,128)(2,1)S(1)}, u32[]{:S(2)}, u32[]{:S(2)}) %collective-permute-start) | collective-permute-done | bytes 884768 | tf_op jit(solution)/shard_map/ppermute | solution.py:12
  59.7 1.0 fusion.8
  60.7 0.0 collective-permute-done.3
  60.7 0.7 convolution_add_fusion
  61.3 4.1 %collective-permute-start.4 = (f32[384,1152]{1,0:T(8,128)S(1)}, f32[384,1152]{1,0:T(8,128)S(1)}, u32[]{:S(2)}, u32[]{:S(2)}) collective-permute-start(f32[384,1152]{1,0:T(8,128)S(1)} %convolution_add_fusion), channel_id=1, source_target_pairs={{0,1},{1,2},{2,3},{3,4},{4,5},{5,6},{6,7},{7,8},{8,9},{9,10},{10,1... | collective-permute-start | bytes 5308424 | tf_op jit(solution)/shard_map/ppermute | solution.py:12
  65.5 10.8 %collective-permute-start.1 = (bf16[384,1152]{1,0:T(8,128)(2,1)S(1)}, bf16[384,1152]{1,0:T(8,128)(2,1)S(1)}, u32[]{:S(2)}, u32[]{:S(2)}) collective-permute-start(bf16[384,1152]{1,0:T(8,128)(2,1)S(1)} %collective-permute-done), channel_id=1, source_target_pairs={{0,1},{1,2},{2,3},{3,4},{4,5},{5,6},{6,7},{7,8},{8,9},{9,10},{10,1... | collective-permute-start | bytes 2654216 | tf_op jit(solution)/shard_map/ppermute | solution.py:12
  76.3 39.4 %collective-permute-done.1 = bf16[384,1152]{1,0:T(8,128)(2,1)S(1)} collective-permute-done((bf16[384,1152]{1,0:T(8,128)(2,1)S(1)}, bf16[384,1152]{1,0:T(8,128)(2,1)S(1)}, u32[]{:S(2)}, u32[]{:S(2)}) %collective-permute-start.1) | collective-permute-done | bytes 884768 | tf_op jit(solution)/shard_map/ppermute | solution.py:12
  115.7 1.0 fusion.9
  116.7 0.7 fusion.13
  117.4 0.0 collective-permute-done.4
  117.4 0.3 add.108
  117.6 4.1 %collective-permute-start.5 = (f32[384,1152]{1,0:T(8,128)S(1)}, f32[384,1152]{1,0:T(8,128)S(1)}, u32[]{:S(2)}, u32[]{:S(2)}) collective-permute-start(f32[384,1152]{1,0:T(8,128)S(1)} %add.108), channel_id=1, source_target_pairs={{0,1},{1,2},{2,3},{3,4},{4,5},{5,6},{6,7},{7,8},{8,9},{9,10},{10,1... | collective-permute-start | bytes 5308424 | tf_op jit(solution)/shard_map/ppermute | solution.py:12
  121.7 16.8 %collective-permute-start.2 = (bf16[384,1152]{1,0:T(8,128)(2,1)S(1)}, bf16[384,1152]{1,0:T(8,128)(2,1)S(1)}, u32[]{:S(2)}, u32[]{:S(2)}) collective-permute-start(bf16[384,1152]{1,0:T(8,128)(2,1)S(1)} %collective-permute-done.1), channel_id=1, source_target_pairs={{0,1},{1,2},{2,3},{3,4},{4,5},{5,6},{6,7},{7,8},{8,9},{9,10},{10,1... | collective-permute-start | bytes 2654216 | tf_op jit(solution)/shard_map/ppermute | solution.py:12
  138.6 0.7 fusion.16
  139.3 0.7 convolution_add_fusion.3
  140.0 31.7 %collective-permute-done.2 = bf16[384,1152]{1,0:T(8,128)(2,1)S(1)} collective-permute-done((bf16[384,1152]{1,0:T(8,128)(2,1)S(1)}, bf16[384,1152]{1,0:T(8,128)(2,1)S(1)}, u32[]{:S(2)}, u32[]{:S(2)}) %collective-permute-start.2) | collective-permute-done | bytes 884768 | tf_op jit(solution)/shard_map/ppermute | solution.py:12
  171.8 1.0 fusion.10
  172.7 0.7 fusion.14
  173.4 0.0 collective-permute-done.5
  173.4 0.2 add.109
  173.6 0.0 copy-start.1
  173.6 37.7 %collective-permute-start.6 = (f32[384,1152]{1,0:T(8,128)S(1)}, f32[384,1152]{1,0:T(8,128)S(1)}, u32[]{:S(2)}, u32[]{:S(2)}) collective-permute-start(f32[384,1152]{1,0:T(8,128)S(1)} %add.109), channel_id=1, source_target_pairs={{0,765},{1,766},{2,767},{3,0},{4,1},{5,2},{6,3},{7,4},{8,5},{9,6},... | collective-permute-start | bytes 5308424 | tf_op jit(solution)/shard_map/ppermute | solution.py:12
  211.3 0.7 convolution_add_fusion.2
  212.0 0.6 add_multiply_fusion
  212.6 0.0 copy-done.1
  212.6 1.0 multiply_reduce_fusion.1
  213.6 1.3 divide_convert_fusion.1
  214.9 30.7 %collective-permute-done.6 = f32[384,1152]{1,0:T(8,128)S(1)} collective-permute-done((f32[384,1152]{1,0:T(8,128)S(1)}, f32[384,1152]{1,0:T(8,128)S(1)}, u32[]{:S(2)}, u32[]{:S(2)}) %collective-permute-start.6) | collective-permute-done | bytes 1769504 | tf_op jit(solution)/shard_map/ppermute | solution.py:12
  245.6 0.4 multiply_reduce_fusion
  246.0 1.3 divide_convert_fusion
  (2 shorter events, 0.0 us)
Async XLA Ops:
  0.6 3.6 %copy-start = (bf16[384,1152]{1,0:T(8,128)(2,1)S(1)}, bf16[384,1152]{1,0:T(8,128)(2,1)}, u32[]{:S(2)}) copy-start(bf16[384,1152]{1,0:T(8,128)(2,1)} %param.5) | copy-start | bytes 2654212
  7.1 53.6 %collective-permute-start.3 = (f32[384,1152]{1,0:T(8,128)S(1)}, f32[384,1152]{1,0:T(8,128)S(1)}, u32[]{:S(2)}, u32[]{:S(2)}) collective-permute-start(f32[384,1152]{1,0:T(8,128)S(1)} %fusion.15), channel_id=1, source_target_pairs={{0,1},{1,2},{2,3},{3,4},{4,5},{5,6},{6,7},{7,8},{8,9},{9,10},{10,1... | collective-permute-start | bytes 5308424 | tf_op jit(solution)/shard_map/ppermute | solution.py:12
  11.1 48.6 %collective-permute-start = (bf16[384,1152]{1,0:T(8,128)(2,1)S(1)}, bf16[384,1152]{1,0:T(8,128)(2,1)S(1)}, u32[]{:S(2)}, u32[]{:S(2)}) collective-permute-start(bf16[384,1152]{1,0:T(8,128)(2,1)S(1)} %fusion.12), channel_id=1, source_target_pairs={{0,1},{1,2},{2,3},{3,4},{4,5},{5,6},{6,7},{7,8},{8,9},{9,10},{10,1... | collective-permute-start | bytes 2654216 | tf_op jit(solution)/shard_map/ppermute | solution.py:12
  61.3 56.0 %collective-permute-start.4 = (f32[384,1152]{1,0:T(8,128)S(1)}, f32[384,1152]{1,0:T(8,128)S(1)}, u32[]{:S(2)}, u32[]{:S(2)}) collective-permute-start(f32[384,1152]{1,0:T(8,128)S(1)} %convolution_add_fusion), channel_id=1, source_target_pairs={{0,1},{1,2},{2,3},{3,4},{4,5},{5,6},{6,7},{7,8},{8,9},{9,10},{10,1... | collective-permute-start | bytes 5308424 | tf_op jit(solution)/shard_map/ppermute | solution.py:12
  65.5 50.3 %collective-permute-start.1 = (bf16[384,1152]{1,0:T(8,128)(2,1)S(1)}, bf16[384,1152]{1,0:T(8,128)(2,1)S(1)}, u32[]{:S(2)}, u32[]{:S(2)}) collective-permute-start(bf16[384,1152]{1,0:T(8,128)(2,1)S(1)} %collective-permute-done), channel_id=1, source_target_pairs={{0,1},{1,2},{2,3},{3,4},{4,5},{5,6},{6,7},{7,8},{8,9},{9,10},{10,1... | collective-permute-start | bytes 2654216 | tf_op jit(solution)/shard_map/ppermute | solution.py:12
  117.6 55.8 %collective-permute-start.5 = (f32[384,1152]{1,0:T(8,128)S(1)}, f32[384,1152]{1,0:T(8,128)S(1)}, u32[]{:S(2)}, u32[]{:S(2)}) collective-permute-start(f32[384,1152]{1,0:T(8,128)S(1)} %add.108), channel_id=1, source_target_pairs={{0,1},{1,2},{2,3},{3,4},{4,5},{5,6},{6,7},{7,8},{8,9},{9,10},{10,1... | collective-permute-start | bytes 5308424 | tf_op jit(solution)/shard_map/ppermute | solution.py:12
  121.7 50.0 %collective-permute-start.2 = (bf16[384,1152]{1,0:T(8,128)(2,1)S(1)}, bf16[384,1152]{1,0:T(8,128)(2,1)S(1)}, u32[]{:S(2)}, u32[]{:S(2)}) collective-permute-start(bf16[384,1152]{1,0:T(8,128)(2,1)S(1)} %collective-permute-done.1), channel_id=1, source_target_pairs={{0,1},{1,2},{2,3},{3,4},{4,5},{5,6},{6,7},{7,8},{8,9},{9,10},{10,1... | collective-permute-start | bytes 2654216 | tf_op jit(solution)/shard_map/ppermute | solution.py:12
  173.6 39.0 %copy-start.1 = (bf16[384,1152]{1,0:T(8,128)(2,1)S(1)}, bf16[384,1152]{1,0:T(8,128)(2,1)}, u32[]{:S(2)}) copy-start(bf16[384,1152]{1,0:T(8,128)(2,1)} %param.4) | copy-start | bytes 2654212
  173.6 72.0 %collective-permute-start.6 = (f32[384,1152]{1,0:T(8,128)S(1)}, f32[384,1152]{1,0:T(8,128)S(1)}, u32[]{:S(2)}, u32[]{:S(2)}) collective-permute-start(f32[384,1152]{1,0:T(8,128)S(1)} %add.109), channel_id=1, source_target_pairs={{0,765},{1,766},{2,767},{3,0},{4,1},{5,2},{6,3},{7,4},{8,5},{9,6},... | collective-permute-start | bytes 5308424 | tf_op jit(solution)/shard_map/ppermute | solution.py:12
where the time goes:
time: 248 us; the launch traced here: 247 us
  waiting for transfers between devices  147 us (59%)
  starting transfers between devices  81.2 us (33%)
  matrix products  9.68 us (4%)
  other arithmetic  7.49 us (3%)
    ppermute x7, waiting for transfers between devices, from_behind(): return lax.ppermute(value, axis, pairs)  147 us
    ppermute x7, starting transfers between devices, from_behind(): return lax.ppermute(value, axis, pairs)  81.2 us
  transfers between devices with their start and end apart: 7, of which 4 were waited for; matrix products, arithmetic and copies ran while one was open for 4% of the time, Pallas kernels for 0%

commit v1 on v0

v1 whole, which is shorter than its diff:
```python
import functools
import jax
import jax.numpy as jnp
from jax import lax
from jax.experimental import pallas as pl
from jax.experimental.pallas import tpu as pltpu
from jax.sharding import PartitionSpec as P

MESH = pl.DeviceIdType.MESH
D = 1152
ROWS = 384
SPAN = 4
R = 128
NC = ROWS // R
WIDE = 256
LOG2E = 1.4426950408889634

P1, P2, P3, Q1, Q2, Q3 = 1, 2, 3, 5, 6, 7


def digits(*order):
    code = 0
    for digit in reversed(order):
        code = code * 8 + digit
    return code


ORDER = {
    (1, 0): digits(Q2, P1, Q1, P3, Q3, P2),
    (1, 1): digits(Q2, P1, Q1, Q3, P3, P2),
    (0, 0): digits(Q2, P1, Q3, P3, Q1, P2),
    (0, 1): digits(Q2, P1, Q3, Q1, P3, P2),
}


def place(index, total):
    index = lax.rem(index + total, total)
    return (lax.div(index, 2), lax.rem(index, 2))


def entries(dots, scale, bias, sign=None):
    power = dots * (scale * LOG2E) + bias * LOG2E
    if sign is not None:
        power = power * sign
    grown = jnp.exp2(power)
    one = 1.0 + grown
    inverse = pl.reciprocal(one, approx=True)
    inverse = inverse * (2.0 - one * inverse)
    term = jnp.where(grown < 0.0078125, grown * (1.0 - grown * (0.5 - grown * (1.0 / 3.0))), jnp.log(one))
    coef = grown * inverse * scale
    if sign is not None:
        coef = coef * sign
    return term, coef.astype(jnp.bfloat16)


def lanes(term):
    folded = term[:, :R]
    for j in range(R, term.shape[1], R):
        folded = folded + term[:, j : j + R]
    return folded


def kernel(total, scaling, shift, picture, caption, loss_out, image_out, text_out,
           raw, buf, grad, loss, inv, in_sem, send_sem, recv_sem, ack):
    blk, inner_index = lax.axis_index("blk"), lax.axis_index("inner")
    me = blk * 2 + inner_index
    core = lax.rem(blk, 2)
    p = core
    q = 1 - core
    sgn = 1 - 2 * core
    outer = 1 - (core - inner_index) * (core - inner_index)

    barrier = pltpu.get_barrier_semaphore()
    for away in (1, 2, 3):
        pl.semaphore_signal(barrier, inc=1, device_id=place(me - away, total), device_id_type=MESH)

    def fetch(kind, c):
        ref = caption if kind == 0 else picture
        rows = pl.ds(c * R, R)
        return pltpu.make_async_copy(ref.at[rows], raw.at[kind, rows], in_sem.at[kind, c])

    for c in range(NC):
        for kind in (0, 1):
            fetch(kind, c).start()

    def chunk(kind, distance, c):
        start = c * R if isinstance(c, int) else pl.multiple_of(c * R, R)
        return buf.at[kind, distance, pl.ds(start, R)]

    def send(slot, kind, source, target, away, c):
        return pltpu.make_async_remote_copy(
            src_ref=chunk(kind, source, c),
            dst_ref=chunk(kind, target, c),
            send_sem=send_sem.at[slot, c],
            recv_sem=recv_sem.at[kind, target, c],
            device_id=place(me + away, total),
            device_id_type=MESH,
        )

    def s0(c):
        return send(0, p, 0, 1, sgn, c)

    def s1(c):
        return send(1, p, 0, 2, 2 * sgn, c)

    def s2(c):
        return send(2, q, 0, 1, -sgn, c)

    def s3(c):
        return send(3, p, 1, 3, 2 * sgn, c)

    def s4(c):
        return send(4, p, outer, 3 - outer, sgn * (3 - 2 * outer), c)

    def s5(c):
        return send(5, q, outer, 3 - outer, -sgn * (3 - 2 * outer), c)

    def start(*sends):
        for one in sends:
            for c in range(NC):
                one(c).start()

    for c in range(NC):
        rows = pl.ds(c * R, R)
        for kind in (0, 1):
            fetch(kind, c).wait()
            values = raw[kind, rows].astype(jnp.float32)
            shrink = 1.0 / jnp.sqrt(jnp.sum(values * values, axis=-1, keepdims=True) + 1e-06)
            inv[kind, rows] = shrink
            buf[kind, 0, rows] = (values * shrink).astype(jnp.bfloat16)

    pl.semaphore_wait(barrier, 3)
    for away in (1, 2, 3):
        pl.semaphore_signal(ack.at[away - 1], inc=1, device_id=place(me + away, total), device_id_type=MESH)

    on_first, on_second = core == 0, core == 1
    is_outer, is_inner = outer == 1, outer == 0

    @pl.when(on_first & is_outer)
    def _():
        start(s0)

    @pl.when(on_first & is_inner)
    def _():
        start(s4)

    @pl.when(on_first)
    def _():
        start(s1)

    @pl.when(on_second)
    def _():
        start(s2)

    @pl.when(on_second & is_inner)
    def _():
        start(s5)

    pl.semaphore_wait(ack.at[0], 1)

    @pl.when(on_first)
    def _():
        start(s2)

    @pl.when((on_first & is_inner) | on_second)
    def _():
        start(s0)

    scale, bias = scaling[0], shift[0]

    row = lax.broadcasted_iota(jnp.int32, (ROWS, ROWS), 0)
    col = lax.broadcasted_iota(jnp.int32, (ROWS, ROWS), 1)
    sign = jnp.where(row == col, jnp.float32(-1.0), jnp.float32(1.0))
    dots = lax.dot_general(buf[1, 0], buf[0, 0], (((1,), (1,)), ((), ())), preferred_element_type=jnp.float32)
    term, coef = entries(dots, scale, bias, sign)
    loss[0] = lanes(term)
    loss[1] = jnp.zeros((ROWS, R), jnp.float32)
    for n in range(0, D, 384):
        cols = pl.ds(n, 384)
        grad[1, :, cols] = jnp.dot(coef, buf[0, 0, :, cols], preferred_element_type=jnp.float32)
        grad[0, :, cols] = lax.dot_general(coef, buf[1, 0, :, cols], (((0,), (0,)), ((), ())), preferred_element_type=jnp.float32)

    pl.semaphore_wait(ack.at[1], 1)

    @pl.when(on_second)
    def _():
        start(s1)

    pl.semaphore_wait(ack.at[2], 1)

    @pl.when(on_first & is_inner)
    def _():
        start(s5)

    @pl.when(on_second & is_inner)
    def _():
        start(s4)

    def arrived(kind, distance, c):
        pltpu.make_async_remote_copy(
            src_ref=chunk(kind, distance, c), dst_ref=chunk(kind, distance, c),
            send_sem=send_sem.at[0, c], recv_sem=recv_sem.at[kind, distance, c],
            device_id=place(me + 1, total), device_id_type=MESH).wait_recv()

    def use(digit, first, count):
        second = lax.div(digit, 4)
        distance = lax.rem(digit, 4)
        kind = p + second * (q - p)
        other = 1 - kind
        for c in range(first, first + count):
            arrived(kind, distance, c)

            @pl.when(digit == P1)
            def _():
                s3(c).start()

            @pl.when((digit == P1) & is_outer)
            def _():
                s4(c).start()

            @pl.when((digit == Q1) & is_outer)
            def _():
                s5(c).start()

        far = buf.at[kind, distance, pl.ds(first * R, count * R)]
        dots = lax.dot_general(buf[other, 0], far[...], (((1,), (1,)), ((), ())), preferred_element_type=jnp.float32)
        term, coef = entries(dots, scale, bias)
        loss[kind] += lanes(term)
        for n in range(0, D, 384):
            cols = pl.ds(n, 384)
            grad[other, :, cols] += jnp.dot(coef, far[:, cols], preferred_element_type=jnp.float32)

    split = 2 + outer + (1 - core)

    def each(first, count):
        def body(_, code):
            use(lax.rem(code, 8), first, count)
            return lax.div(code, 8)
        return body

    code = 0
    for (o, c), value in ORDER.items():
        here = (1 - (outer - o) * (outer - o)) * (1 - (core - c) * (core - c))
        code = code + here * value

    def group(g, code):
        steps = lax.div(2 - g, 2) + lax.rem(g, 2) * split + lax.div(g, 2) * (5 - split)
        lax.fori_loop(0, steps, each(0, WIDE // R), code)
        return lax.fori_loop(0, steps, each(WIDE // R, NC - WIDE // R), code)

    lax.fori_loop(0, 3, group, code)

    for kind, ref in ((0, text_out), (1, image_out)):
        for r in range(0, ROWS, 32):
            rows = pl.ds(r, 32)
            values = raw[kind, rows].astype(jnp.float32)
            shrink = inv[kind, rows]
            whole = grad[kind, rows]
            along = jnp.sum(values * whole, axis=-1, keepdims=True) * (shrink * shrink)
            ref[rows] = ((whole - values * along) * shrink).astype(jnp.bfloat16)
    loss_out[...] = jnp.sum(loss[0].T, axis=0, keepdims=True) * (1.0 / (SPAN * ROWS))

    for c in range(NC):
        for one in (s0, s1, s2, s3, s4, s5):
            one(c).wait_send()


def local(picture, caption, scaling, shift):
    total = lax.axis_size("blk") * lax.axis_size("inner")
    vmem = pl.BlockSpec(memory_space=pltpu.VMEM)
    smem = pl.BlockSpec(memory_space=pltpu.SMEM)
    hbm = pl.BlockSpec(memory_space=pltpu.HBM)
    loss, image, text = pl.pallas_call(
        functools.partial(kernel, total),
        out_shape=(
            jax.ShapeDtypeStruct((1, ROWS), jnp.float32),
            jax.ShapeDtypeStruct((ROWS, D), jnp.bfloat16),
            jax.ShapeDtypeStruct((ROWS, D), jnp.bfloat16),
        ),
        in_specs=[smem, smem, hbm, hbm],
        out_specs=(vmem, vmem, vmem),
        scratch_shapes=[
            pltpu.VMEM((2, ROWS, D), jnp.bfloat16),
            pltpu.VMEM((2, 4, ROWS, D), jnp.bfloat16),
            pltpu.VMEM((2, ROWS, D), jnp.float32),
            pltpu.VMEM((2, ROWS, R), jnp.float32),
            pltpu.VMEM((2, ROWS, 1), jnp.float32),
            pltpu.SemaphoreType.DMA((2, NC)),
            pltpu.SemaphoreType.DMA((6, NC)),
            pltpu.SemaphoreType.DMA((2, 4, NC)),
            pltpu.SemaphoreType.REGULAR((3,)),
        ],
        compiler_params=pltpu.CompilerParams(collective_id=0, has_side_effects=True, vmem_limit_bytes=40 * 2**20),
    )(scaling.reshape(1), shift.reshape(1), picture, caption)
    return loss.reshape(ROWS), image, text


def solution(mesh):
    in_specs = (P(("blk", "inner"), None), P(("blk", "inner"), None), P(), P())
    out_specs = (P(("blk", "inner")), P(("blk", "inner"), None), P(("blk", "inner"), None))
    return jax.shard_map(local, mesh=mesh, in_specs=in_specs, out_specs=out_specs, check_vma=False)
```

time: 248 us -> 58.7 us (0.24)
  waiting for transfers between devices: 147 us -> 0 us
  starting transfers between devices: 81.2 us -> 0 us
  Pallas kernels: 0 us -> 51.7 us
  matrix products: 9.68 us -> 0 us
  other arithmetic: 7.49 us -> 0.6 us
  local copies, waits for them, and re-layouts: 0.01 us -> 4.15 us
    ppermute x7 -> x0, waiting for transfers between devices: 147 us -> none  [from_behind(): return lax.ppermute(value, axis, pairs)]
    ppermute x7 -> x0, starting transfers between devices: 81.2 us -> none  [from_behind(): return lax.ppermute(value, axis, pairs)]
    pallas_call x0 -> x1, Pallas kernels: none -> 51.7 us  [local(): pl.pallas_call(functools.partial(kernel, total), out_shape=(jax.ShapeDtyp...]
    dot_general x12 -> x0, matrix products: 9.68 us -> none  [the longest x4 3.93 us: matrix_entries(): lax.dot_general(picture_summed, caption_summed, (((1,), (1,)), ((), ())),...]
    convert_element_type x4 -> x0, other arithmetic: 4.37 us -> none  [the longest x1 1.44 us: local(): picture_summed = image_unit.astype(jnp.bfloat16)]
    unnamed x4 -> x6, local copies, waits for them, and re-layouts: 0.01 us -> 4.15 us
  transfers between devices with their start and end apart: 7 -> 0, of which waited for: 4 -> 0; matrix products, arithmetic and copies ran while one was open for 4% -> 0% of each run, Pallas kernels for 0% -> 0%
where the time goes in v1:
time: 58.7 us; the launch traced here: 58.4 us
  Pallas kernels  51.7 us (88%)
  local copies, waits for them, and re-layouts  4.15 us (7%)
  between operations  1.94 us (3%)
  other arithmetic  0.6 us (1%)
    pallas_call x1, Pallas kernels, local(): pl.pallas_call(functools.partial(kernel, total), out_shape=(jax.ShapeDtyp...  51.7 us
    unnamed x6, local copies, waits for them, and re-layouts  4.15 us

profile of v1, /device:TPU:1, one launch (start us, length us, event | category | flops | bytes accessed | tf_op | source)
XLA Modules:
  0.0 58.4 jit_solution(10576521656976667921)
XLA Ops:
  1.9 0.0 copy-start
  1.9 1.2 %copy-done = bf16[384,1152]{1,0:T(8,128)(2,1)S(1)} copy-done((bf16[384,1152]{1,0:T(8,128)(2,1)S(1)}, bf16[384,1152]{1,0:T(8,128)(2,1)}, u32[]{:S(2)}) %copy-start) | copy-done | bytes 884760
  3.1 0.0 copy-start.1
  3.1 1.2 %copy-done.1 = bf16[384,1152]{1,0:T(8,128)(2,1)S(1)} copy-done((bf16[384,1152]{1,0:T(8,128)(2,1)S(1)}, bf16[384,1152]{1,0:T(8,128)(2,1)}, u32[]{:S(2)}) %copy-start.1) | copy-done | bytes 884760
  4.3 51.7 %shard_map.67 = (f32[1,384]{1,0:T(1,128)S(1)}, bf16[384,1152]{1,0:T(8,128)(2,1)S(1)}, bf16[384,1152]{1,0:T(8,128)(2,1)S(1)}) custom-call(f32[1]{0:T(128)} %bitcast.2.scaling, f32[1]{0:T(128)} %bitcast.3.shift, bf16[384,1152]{1,0:T(8,128)(2,1)S(1)} %copy-done, bf16[384,1152]{1,0:T(8,128)(2,1)S(1)} %copy-done.1), custom_call_target="tpu_custom_call" | custom-call | tf_op jit(solution)/shard_map/pallas_call | solution.py:273
  55.9 0.6 %reduce = f32[384]{0:T(512)} reduce(f32[1,384]{1,0:T(1,128)S(1)} %get-tuple-element.6, f32[]{:T(128)} %constant.2), dimensions={0}, to_apply=%get-tuple-element.6.reduce_sub_computation | reduce | bytes 3076 | tf_op jit(solution)/shard_map/pallas_call | solution.py:273
  56.5 0.9 %copy.11 = bf16[384,1152]{1,0:T(8,128)(2,1)} copy(bf16[384,1152]{1,0:T(8,128)(2,1)S(1)} %get-tuple-element.13) | data formatting | bytes 1769472
  57.5 0.9 %copy.12 = bf16[384,1152]{1,0:T(8,128)(2,1)} copy(bf16[384,1152]{1,0:T(8,128)(2,1)S(1)} %get-tuple-element.14) | data formatting | bytes 1769472
Async XLA Ops:
  1.9 1.2 %copy-start = (bf16[384,1152]{1,0:T(8,128)(2,1)S(1)}, bf16[384,1152]{1,0:T(8,128)(2,1)}, u32[]{:S(2)}) copy-start(bf16[384,1152]{1,0:T(8,128)(2,1)} %picture.1) | copy-start | bytes 2654212
  3.1 1.2 %copy-start.1 = (bf16[384,1152]{1,0:T(8,128)(2,1)S(1)}, bf16[384,1152]{1,0:T(8,128)(2,1)}, u32[]{:S(2)}) copy-start(bf16[384,1152]{1,0:T(8,128)(2,1)} %caption.1) | copy-start | bytes 2654212

commit v2 on v1

--- a/solution.py
+++ b/solution.py
@@ -16,21 +16,25 @@
 LOG2E = 1.4426950408889634
 
 P1, P2, P3, Q1, Q2, Q3 = 1, 2, 3, 5, 6, 7
-
-
-def digits(*order):
-    code = 0
-    for digit in reversed(order):
-        code = code * 8 + digit
-    return code
-
-
-ORDER = {
-    (1, 0): digits(Q2, P1, Q1, P3, Q3, P2),
-    (1, 1): digits(Q2, P1, Q1, Q3, P3, P2),
-    (0, 0): digits(Q2, P1, Q3, P3, Q1, P2),
-    (0, 1): digits(Q2, P1, Q3, Q1, P3, P2),
-}
+LATE = 8
+
+
+def packed(*items):
+    codes = []
+    for begin in range(0, len(items), 6):
+        code = 0
+        for item in reversed(items[begin : begin + 6]):
+            code = code * 16 + item
+        codes.append(code)
+    return codes
+
+
+OUTER = packed(Q2, LATE + Q2, Q1, Q3, P1, LATE + Q1, LATE + Q3, LATE + P1, P3, LATE + P3, P2, LATE + P2)
+ACROSS = packed(Q2, LATE + Q2, P3, LATE + P3, P1, LATE + P1, Q3, LATE + Q3, Q1, P2, LATE + Q1, LATE + P2)
+ALONG = packed(Q2, LATE + Q2, P1, LATE + P1, Q3, LATE + Q3, Q1, P2, P3, LATE + Q1, LATE + P2, LATE + P3)
+
+EARLIEST = 2
+FIRST_IN = packed(Q2, LATE + Q2, P1, LATE + P1, P3, LATE + P3, Q1, LATE + Q1, P2, Q3, LATE + Q3, LATE + P2)
 
 
 def place(index, total):
@@ -60,8 +64,8 @@
     return folded
 
 
-def kernel(total, scaling, shift, picture, caption, loss_out, image_out, text_out,
-           raw, buf, grad, loss, inv, in_sem, send_sem, recv_sem, ack):
+def kernel(total, scaling_in, shift_in, picture, caption, loss_out, image_out, text_out,
+           raw, buf, grad, loss, inv, in_sem, send_sem, recv_sem, ack, scalars, scalar_sem):
     blk, inner_index = lax.axis_index("blk"), lax.axis_index("inner")
     me = blk * 2 + inner_index
     core = lax.rem(blk, 2)
@@ -74,6 +78,12 @@
     for away in (1, 2, 3):
         pl.semaphore_signal(barrier, inc=1, device_id=place(me - away, total), device_id_type=MESH)
 
+    fetch_scalars = [
+        pltpu.make_async_copy(ref, scalars.at[i], scalar_sem.at[i]) for i, ref in enumerate((scaling_in, shift_in))
+    ]
+    for one in fetch_scalars:
+        one.start()
+
     def fetch(kind, c):
         ref = caption if kind == 0 else picture
         rows = pl.ds(c * R, R)
@@ -81,7 +91,7 @@
 
     for c in range(NC):
         for kind in (0, 1):
-            fetch(kind, c).start()
+            fetch(kind, c).start( )
 
     def chunk(kind, distance, c):
         start = c * R if isinstance(c, int) else pl.multiple_of(c * R, R)
@@ -120,53 +130,74 @@
             for c in range(NC):
                 one(c).start()
 
-    for c in range(NC):
+    def normalize(kind, c):
+        fetch(kind, c).wait()
         rows = pl.ds(c * R, R)
-        for kind in (0, 1):
-            fetch(kind, c).wait()
-            values = raw[kind, rows].astype(jnp.float32)
-            shrink = 1.0 / jnp.sqrt(jnp.sum(values * values, axis=-1, keepdims=True) + 1e-06)
-            inv[kind, rows] = shrink
-            buf[kind, 0, rows] = (values * shrink).astype(jnp.bfloat16)
-
-    pl.semaphore_wait(barrier, 3)
-    for away in (1, 2, 3):
-        pl.semaphore_signal(ack.at[away - 1], inc=1, device_id=place(me + away, total), device_id_type=MESH)
-
+        values = raw[kind, rows].astype(jnp.float32)
+        shrink = 1.0 / jnp.sqrt(jnp.sum(values * values, axis=-1, keepdims=True) + 1e-06)
+        inv[kind, rows] = shrink
+        buf[kind, 0, rows] = (values * shrink).astype(jnp.bfloat16)
+
+    high = lax.rem(lax.div(blk, 2), 2)
+    along = (high - core) * (high - core)
     on_first, on_second = core == 0, core == 1
     is_outer, is_inner = outer == 1, outer == 0
 
-    @pl.when(on_first & is_outer)
+    for c in range(NC):
+        normalize(0, c)
+        if c == 0:
+            pl.semaphore_wait(barrier, 3)
+            for away in (1, 2, 3):
+                pl.semaphore_signal(ack.at[away - 1], inc=1, device_id=place(me + away, total), device_id_type=MESH)
+
+        @pl.when(on_first & is_outer)
+        def _():
+            s0(c).start()
+
+        @pl.when(on_first & is_inner & (along == 0))
+        def _():
+            s4(c).start()
+
+        @pl.when(on_second)
+        def _():
+            s2(c).start()
+
+        normalize(1, c)
+
+    @pl.when(on_second & is_inner)
+    def _():
+        start(s5)
+
+    @pl.when(on_first)
+    def _():
+        start(s1)
+
+    ahead_first = me == EARLIEST - 1
+
+    @pl.when(ahead_first)
     def _():
         start(s0)
 
-    @pl.when(on_first & is_inner)
-    def _():
-        start(s4)
+    pl.semaphore_wait(ack.at[0], 1)
 
     @pl.when(on_first)
     def _():
-        start(s1)
-
-    @pl.when(on_second)
-    def _():
         start(s2)
 
-    @pl.when(on_second & is_inner)
-    def _():
+    @pl.when((on_first & is_inner & jnp.logical_not(ahead_first)) | on_second)
+    def _():
+        start(s0)
+
+    third_now = is_inner & on_first & (along == 1)
+
+    @pl.when(third_now)
+    def _():
+        pl.semaphore_wait(ack.at[2], 1)
         start(s5)
 
-    pl.semaphore_wait(ack.at[0], 1)
-
-    @pl.when(on_first)
-    def _():
-        start(s2)
-
-    @pl.when((on_first & is_inner) | on_second)
-    def _():
-        start(s0)
-
-    scale, bias = scaling[0], shift[0]
+    for one in fetch_scalars:
+        one.wait()
+    scale, bias = scalars[0, 0], scalars[1, 0]
 
     row = lax.broadcasted_iota(jnp.int32, (ROWS, ROWS), 0)
     col = lax.broadcasted_iota(jnp.int32, (ROWS, ROWS), 1)
@@ -186,15 +217,18 @@
     def _():
         start(s1)
 
-    pl.semaphore_wait(ack.at[2], 1)
-
-    @pl.when(on_first & is_inner)
-    def _():
-        start(s5)
-
-    @pl.when(on_second & is_inner)
-    def _():
-        start(s4)
+    def late_sends():
+        @pl.when(jnp.logical_not(third_now))
+        def _():
+            pl.semaphore_wait(ack.at[2], 1)
+
+        @pl.when(is_inner & ((along == 1) | on_second))
+        def _():
+            start(s4)
+
+        @pl.when(is_inner & on_first & (along == 0))
+        def _():
+            start(s5)
 
     def arrived(kind, distance, c):
         pltpu.make_async_remote_copy(
@@ -202,23 +236,23 @@
             send_sem=send_sem.at[0, c], recv_sem=recv_sem.at[kind, distance, c],
             device_id=place(me + 1, total), device_id_type=MESH).wait_recv()
 
-    def use(digit, first, count):
-        second = lax.div(digit, 4)
-        distance = lax.rem(digit, 4)
+    def use(block, first, count):
+        second = lax.div(block, 4)
+        distance = lax.rem(block, 4)
         kind = p + second * (q - p)
         other = 1 - kind
         for c in range(first, first + count):
             arrived(kind, distance, c)
 
-            @pl.when(digit == P1)
+            @pl.when(block == P1)
             def _():
                 s3(c).start()
 
-            @pl.when((digit == P1) & is_outer)
+            @pl.when((block == P1) & is_outer)
             def _():
                 s4(c).start()
 
-            @pl.when((digit == Q1) & is_outer)
+            @pl.when((block == Q1) & is_outer)
             def _():
                 s5(c).start()
 
@@ -230,25 +264,27 @@
             cols = pl.ds(n, 384)
             grad[other, :, cols] += jnp.dot(coef, far[:, cols], preferred_element_type=jnp.float32)
 
-    split = 2 + outer + (1 - core)
-
-    def each(first, count):
-        def body(_, code):
-            use(lax.rem(code, 8), first, count)
-            return lax.div(code, 8)
-        return body
-
-    code = 0
-    for (o, c), value in ORDER.items():
-        here = (1 - (outer - o) * (outer - o)) * (1 - (core - c) * (core - c))
-        code = code + here * value
-
-    def group(g, code):
-        steps = lax.div(2 - g, 2) + lax.rem(g, 2) * split + lax.div(g, 2) * (5 - split)
-        lax.fori_loop(0, steps, each(0, WIDE // R), code)
-        return lax.fori_loop(0, steps, each(WIDE // R, NC - WIDE // R), code)
-
-    lax.fori_loop(0, 3, group, code)
+    for half in (0, 1):
+        code = outer * OUTER[half] + (1 - outer) * (along * ALONG[half] + (1 - along) * ACROSS[half])
+        code = jnp.where(me == EARLIEST, FIRST_IN[half], code)
+
+        def step(i, code):
+            item = lax.rem(code, 16)
+
+            if half == 0:
+                pl.when(i == 2)(late_sends)
+
+            @pl.when(item < LATE)
+            def _():
+                use(item, 0, WIDE // R)
+
+            @pl.when(item >= LATE)
+            def _():
+                use(item - LATE, WIDE // R, NC - WIDE // R)
+
+            return lax.div(code, 16)
+
+        lax.fori_loop(0, 6, step, code)
 
     for kind, ref in ((0, text_out), (1, image_out)):
         for r in range(0, ROWS, 32):
@@ -268,16 +304,17 @@
 def local(picture, caption, scaling, shift):
     total = lax.axis_size("blk") * lax.axis_size("inner")
     vmem = pl.BlockSpec(memory_space=pltpu.VMEM)
-    smem = pl.BlockSpec(memory_space=pltpu.SMEM)
     hbm = pl.BlockSpec(memory_space=pltpu.HBM)
-    loss, image, text = pl.pallas_call(
+    picture = pltpu.with_memory_space_constraint(picture, pltpu.HBM)
+    caption = pltpu.with_memory_space_constraint(caption, pltpu.HBM)
+    results = pl.pallas_call(
         functools.partial(kernel, total),
         out_shape=(
             jax.ShapeDtypeStruct((1, ROWS), jnp.float32),
             jax.ShapeDtypeStruct((ROWS, D), jnp.bfloat16),
             jax.ShapeDtypeStruct((ROWS, D), jnp.bfloat16),
         ),
-        in_specs=[smem, smem, hbm, hbm],
+        in_specs=[hbm] * 4,
         out_specs=(vmem, vmem, vmem),
         scratch_shapes=[
             pltpu.VMEM((2, ROWS, D), jnp.bfloat16),
@@ -289,9 +326,12 @@
             pltpu.SemaphoreType.DMA((6, NC)),
             pltpu.SemaphoreType.DMA((2, 4, NC)),
             pltpu.SemaphoreType.REGULAR((3,)),
+            pltpu.SMEM((2, 1), jnp.float32),
+            pltpu.SemaphoreType.DMA((2,)),
         ],
         compiler_params=pltpu.CompilerParams(collective_id=0, has_side_effects=True, vmem_limit_bytes=40 * 2**20),
     )(scaling.reshape(1), shift.reshape(1), picture, caption)
+    loss, image, text = results
     return loss.reshape(ROWS), image, text
 
 

time: 58.7 us -> 55.1 us (0.939)
  local copies, waits for them, and re-layouts: 4.15 us -> 1.82 us
  Pallas kernels: 51.7 us -> 50.5 us
    unnamed x6 -> x2, local copies, waits for them, and re-layouts: 4.15 us -> 1.82 us
    pallas_call x1, Pallas kernels: 51.7 us -> 50.5 us  [local(): pl.pallas_call(functools.partial(kernel, total), out_shape=(jax.ShapeDtyp...]
where the time goes in v2:
time: 55.1 us; the launch traced here: 54.9 us
  Pallas kernels  50.5 us (92%)
  between operations  1.93 us (4%)
  local copies, waits for them, and re-layouts  1.82 us (3%)
  other arithmetic  0.6 us (1%)
    pallas_call x1, Pallas kernels, local(): pl.pallas_call(functools.partial(kernel, total), out_shape=(jax.ShapeDtyp...  50.5 us
    unnamed x2, local copies, waits for them, and re-layouts  1.82 us

profile of v2, /device:TPU:1, one launch (start us, length us, event | category | flops | bytes accessed | tf_op | source)
XLA Modules:
  0.0 54.9 jit_solution(10227778574808435388)
XLA Ops:
  1.9 50.5 %shard_map.67 = (f32[1,384]{1,0:T(1,128)S(1)}, bf16[384,1152]{1,0:T(8,128)(2,1)S(1)}, bf16[384,1152]{1,0:T(8,128)(2,1)S(1)}) custom-call(f32[1]{0:T(128)} %bitcast.2.scaling_in, f32[1]{0:T(128)} %bitcast.3.shift_in, bf16[384,1152]{1,0:T(8,128)(2,1)} %picture.1, bf16[384,1152]{1,0:T(8,128)(2,1)} %caption.1), custom_call_target="tpu_custom_call" | custom-call | tf_op jit(solution)/shard_map/pallas_call | solution.py:310
  52.5 0.6 %reduce = f32[384]{0:T(512)} reduce(f32[1,384]{1,0:T(1,128)S(1)} %get-tuple-element.6, f32[]{:T(128)} %constant.2), dimensions={0}, to_apply=%get-tuple-element.6.reduce_sub_computation | reduce | bytes 3076 | tf_op jit(solution)/shard_map/pallas_call | solution.py:310
  53.1 0.9 %copy.11 = bf16[384,1152]{1,0:T(8,128)(2,1)} copy(bf16[384,1152]{1,0:T(8,128)(2,1)S(1)} %get-tuple-element.13) | data formatting | bytes 1769472
  54.0 0.9 %copy.12 = bf16[384,1152]{1,0:T(8,128)(2,1)} copy(bf16[384,1152]{1,0:T(8,128)(2,1)S(1)} %get-tuple-element.14) | data formatting | bytes 1769472

commit v3 on v2

--- a/solution.py
+++ b/solution.py
@@ -65,7 +65,7 @@
 
 
 def kernel(total, scaling_in, shift_in, picture, caption, loss_out, image_out, text_out,
-           raw, buf, grad, loss, inv, in_sem, send_sem, recv_sem, ack, scalars, scalar_sem):
+           raw, buf, grad, loss, inv, in_sem, send_sem, recv_sem, ack):
     blk, inner_index = lax.axis_index("blk"), lax.axis_index("inner")
     me = blk * 2 + inner_index
     core = lax.rem(blk, 2)
@@ -77,12 +77,6 @@
     barrier = pltpu.get_barrier_semaphore()
     for away in (1, 2, 3):
         pl.semaphore_signal(barrier, inc=1, device_id=place(me - away, total), device_id_type=MESH)
-
-    fetch_scalars = [
-        pltpu.make_async_copy(ref, scalars.at[i], scalar_sem.at[i]) for i, ref in enumerate((scaling_in, shift_in))
-    ]
-    for one in fetch_scalars:
-        one.start()
 
     def fetch(kind, c):
         ref = caption if kind == 0 else picture
@@ -195,9 +189,7 @@
         pl.semaphore_wait(ack.at[2], 1)
         start(s5)
 
-    for one in fetch_scalars:
-        one.wait()
-    scale, bias = scalars[0, 0], scalars[1, 0]
+    scale, bias = scaling_in[:1, :1], shift_in[:1, :1]
 
     row = lax.broadcasted_iota(jnp.int32, (ROWS, ROWS), 0)
     col = lax.broadcasted_iota(jnp.int32, (ROWS, ROWS), 1)
@@ -299,6 +291,18 @@
     for c in range(NC):
         for one in (s0, s1, s2, s3, s4, s5):
             one(c).wait_send()
+
+
+def hand_over(loss, image, text, loss_out, image_out, text_out, sem):
+    copies = [
+        pltpu.make_async_copy(source, target, sem.at[i])
+        for i, (source, target) in enumerate(((image, image_out), (text, text_out)))
+    ]
+    for copy in copies:
+        copy.start()
+    loss_out[...] = loss[0]
+    for copy in copies:
+        copy.wait()
 
 
 def local(picture, caption, scaling, shift):
@@ -314,7 +318,7 @@
             jax.ShapeDtypeStruct((ROWS, D), jnp.bfloat16),
             jax.ShapeDtypeStruct((ROWS, D), jnp.bfloat16),
         ),
-        in_specs=[hbm] * 4,
+        in_specs=[vmem, vmem, hbm, hbm],
         out_specs=(vmem, vmem, vmem),
         scratch_shapes=[
             pltpu.VMEM((2, ROWS, D), jnp.bfloat16),
@@ -326,13 +330,24 @@
             pltpu.SemaphoreType.DMA((6, NC)),
             pltpu.SemaphoreType.DMA((2, 4, NC)),
             pltpu.SemaphoreType.REGULAR((3,)),
-            pltpu.SMEM((2, 1), jnp.float32),
-            pltpu.SemaphoreType.DMA((2,)),
         ],
-        compiler_params=pltpu.CompilerParams(collective_id=0, has_side_effects=True, vmem_limit_bytes=40 * 2**20),
-    )(scaling.reshape(1), shift.reshape(1), picture, caption)
-    loss, image, text = results
-    return loss.reshape(ROWS), image, text
+        compiler_params=pltpu.CompilerParams(collective_id=0, allow_input_fusion=[True, True, False, False], has_side_effects=True, vmem_limit_bytes=40 * 2**20),
+    )(jnp.full((8, 128), scaling), jnp.full((8, 128), shift), picture, caption)
+    anywhere = pl.BlockSpec(memory_space=pl.ANY)
+    loss, image, text = pl.pallas_call(
+        hand_over,
+        out_shape=(
+            jax.ShapeDtypeStruct((ROWS,), jnp.float32),
+            jax.ShapeDtypeStruct((ROWS, D), jnp.bfloat16),
+            jax.ShapeDtypeStruct((ROWS, D), jnp.bfloat16),
+        ),
+        in_specs=[vmem, anywhere, anywhere],
+        out_specs=(vmem, hbm, hbm),
+        scratch_shapes=[pltpu.SemaphoreType.DMA((2,))],
+        compiler_params=pltpu.CompilerParams(vmem_limit_bytes=2**20),
+        name="hand_over",
+    )(*results)
+    return loss, image, text
 
 
 def solution(mesh):

time: 55.1 us -> 54.4 us (0.987)
  local copies, waits for them, and re-layouts: 1.82 us -> 0.01 us
  Pallas kernels: 50.5 us -> 52.3 us
  other arithmetic: 0.6 us -> 0 us
    unnamed x2 -> x0, local copies, waits for them, and re-layouts: 1.82 us -> none
    pallas_call x0 -> x1, Pallas kernels: none -> 1.78 us  [local(): pl.pallas_call(hand_over, out_shape=(jax.ShapeDtypeStruct((ROWS,), jnp.fl...]
    pallas_call x1 -> x0, other arithmetic: 0.6 us -> none  [local(): pl.pallas_call(functools.partial(kernel, total), out_shape=(jax.ShapeDtyp...]
where the time goes in v3:
time: 54.4 us; the launch traced here: 54.3 us
  Pallas kernels  52.3 us (96%)
  between operations  1.95 us (4%)
    pallas_call x1, Pallas kernels, local(): pl.pallas_call(functools.partial(kernel, total), out_shape=(jax.ShapeDtyp...  50.5 us
    pallas_call x1, Pallas kernels, local(): pl.pallas_call(hand_over, out_shape=(jax.ShapeDtypeStruct((ROWS,), jnp.fl...  1.78 us

profile of v3, /device:TPU:1, one launch (start us, length us, event | category | flops | bytes accessed | tf_op | source)
XLA Modules:
  0.0 54.3 jit_solution(918074969777014599)
XLA Ops:
  1.9 50.5 %shard_map.67 = (f32[1,384]{1,0:T(1,128)S(1)}, bf16[384,1152]{1,0:T(8,128)(2,1)S(1)}, bf16[384,1152]{1,0:T(8,128)(2,1)S(1)}) custom-call(f32[8,128]{1,0:T(8,128)S(1)} %broadcast_in_dim.6.scaling_in, f32[8,128]{1,0:T(8,128)S(1)} %broadcast_in_dim.7.shift_in, bf16[384,1152]{1,0:T(8,128)(2,1)} %picture.1, bf16[384,1152]{1,0:T(8,128)(2,1)} %caption.1), custom_call_target="tpu_custom_call" | custom-call | tf_op jit(solution)/shard_map/pallas_call | solution.py:314
  52.5 1.8 %hand_over.1 = (f32[384]{0:T(512)}, bf16[384,1152]{1,0:T(8,128)(2,1)}, bf16[384,1152]{1,0:T(8,128)(2,1)}) custom-call(f32[1,384]{1,0:T(1,128)S(1)} %get-tuple-element.6.loss, bf16[384,1152]{1,0:T(8,128)(2,1)S(1)} %get-tuple-element.7.image, bf16[384,1152]{1,0:T(8,128)(2,1)S(1)} %get-tuple-element.8.text), custom_call_target="tpu_custom_call" | custom-call | tf_op jit(solution)/shard_map/hand_over/pallas_call | solution.py:337
  (2 shorter events, 0.0 us)

commit v4 on v3

--- a/solution.py
+++ b/solution.py
@@ -35,6 +35,10 @@
 
 EARLIEST = 2
 FIRST_IN = packed(Q2, LATE + Q2, P1, LATE + P1, P3, LATE + P3, Q1, LATE + Q1, P2, Q3, LATE + Q3, LATE + P2)
+
+ORIGIN = packed(Q2, LATE + Q2, Q3, P1, LATE + Q3, LATE + P1, P3, Q1, LATE + P3, LATE + Q1, P2, LATE + P2)
+
+FOURTH = packed(Q2, LATE + Q2, Q1, P1, LATE + Q1, P3, Q3, LATE + P1, LATE + Q3, LATE + P3, P2, LATE + P2)
 
 
 def place(index, total):
@@ -258,7 +262,7 @@
 
     for half in (0, 1):
         code = outer * OUTER[half] + (1 - outer) * (along * ALONG[half] + (1 - along) * ACROSS[half])
-        code = jnp.where(me == EARLIEST, FIRST_IN[half], code)
+        code = jnp.where(me == EARLIEST, FIRST_IN[half], jnp.where(me == 0, ORIGIN[half], jnp.where(me == 3, FOURTH[half], code)))
 
         def step(i, code):
             item = lax.rem(code, 16)

time: 54.4 us -> 53 us (0.974)
  the two profiles are of different devices: /device:TPU:1 before, /device:TPU:449 now
where the time goes in v4:
time: 53 us; the launch traced here: 52.9 us
  Pallas kernels  50.9 us (96%)
  between operations  1.95 us (4%)
    pallas_call x1, Pallas kernels, local(): pl.pallas_call(functools.partial(kernel, total), out_shape=(jax.ShapeDtyp...  49.1 us
    pallas_call x1, Pallas kernels, local(): pl.pallas_call(hand_over, out_shape=(jax.ShapeDtypeStruct((ROWS,), jnp.fl...  1.78 us

profile of v4, /device:TPU:449, one launch (start us, length us, event | category | flops | bytes accessed | tf_op | source)
XLA Modules:
  0.0 52.9 jit_solution(14208410135222729579)
XLA Ops:
  1.9 49.1 %shard_map.67 = (f32[1,384]{1,0:T(1,128)S(1)}, bf16[384,1152]{1,0:T(8,128)(2,1)S(1)}, bf16[384,1152]{1,0:T(8,128)(2,1)S(1)}) custom-call(f32[8,128]{1,0:T(8,128)S(1)} %broadcast_in_dim.6.scaling_in, f32[8,128]{1,0:T(8,128)S(1)} %broadcast_in_dim.7.shift_in, bf16[384,1152]{1,0:T(8,128)(2,1)} %picture.1, bf16[384,1152]{1,0:T(8,128)(2,1)} %caption.1), custom_call_target="tpu_custom_call" | custom-call | tf_op jit(solution)/shard_map/pallas_call | solution.py:318
  51.1 1.8 %hand_over.1 = (f32[384]{0:T(512)}, bf16[384,1152]{1,0:T(8,128)(2,1)}, bf16[384,1152]{1,0:T(8,128)(2,1)}) custom-call(f32[1,384]{1,0:T(1,128)S(1)} %get-tuple-element.6.loss, bf16[384,1152]{1,0:T(8,128)(2,1)S(1)} %get-tuple-element.7.image, bf16[384,1152]{1,0:T(8,128)(2,1)S(1)} %get-tuple-element.8.text), custom_call_target="tpu_custom_call" | custom-call | tf_op jit(solution)/shard_map/hand_over/pallas_call | solution.py:341
  (2 shorter events, 0.0 us)

commit v5 on v4

--- a/solution.py
+++ b/solution.py
@@ -1,4 +1,5 @@
 import functools
+import math
 import jax
 import jax.numpy as jnp
 from jax import lax
@@ -13,10 +14,13 @@
 R = 128
 NC = ROWS // R
 WIDE = 256
+HALF = 640
 LOG2E = 1.4426950408889634
 
 P1, P2, P3, Q1, Q2, Q3 = 1, 2, 3, 5, 6, 7
 LATE = 8
+BOTH = LATE
+NOTHING = 0
 
 
 def packed(*items):
@@ -31,7 +35,7 @@
 
 OUTER = packed(Q2, LATE + Q2, Q1, Q3, P1, LATE + Q1, LATE + Q3, LATE + P1, P3, LATE + P3, P2, LATE + P2)
 ACROSS = packed(Q2, LATE + Q2, P3, LATE + P3, P1, LATE + P1, Q3, LATE + Q3, Q1, P2, LATE + Q1, LATE + P2)
-ALONG = packed(Q2, LATE + Q2, P1, LATE + P1, Q3, LATE + Q3, Q1, P2, P3, LATE + Q1, LATE + P2, LATE + P3)
+ALONG = packed(Q2, LATE + Q2, P1, LATE + P1, Q3, LATE + Q3, Q1, P2, P3, LATE + Q1, BOTH, NOTHING)
 
 EARLIEST = 2
 FIRST_IN = packed(Q2, LATE + Q2, P1, LATE + P1, P3, LATE + P3, Q1, LATE + Q1, P2, Q3, LATE + Q3, LATE + P2)
@@ -61,6 +65,21 @@
     return term, coef.astype(jnp.bfloat16)
 
 
+def products(near, far, step):
+    total = None
+    for begin in range(0, D, step):
+        width = min(step, D - begin)
+        cols = pl.ds(begin, width)
+        part = lax.dot_general(
+            near[:, cols],
+            far[..., cols].reshape(-1, width),
+            (((1,), (1,)), ((), ())),
+            preferred_element_type=jnp.float32,
+        )
+        total = part if total is None else total + part
+    return total
+
+
 def lanes(term):
     folded = term[:, :R]
     for j in range(R, term.shape[1], R):
@@ -141,6 +160,9 @@
     on_first, on_second = core == 0, core == 1
     is_outer, is_inner = outer == 1, outer == 0
 
+    third_now = is_inner & on_first & (along == 1)
+    prompt = me > EARLIEST
+
     for c in range(NC):
         normalize(0, c)
         if c == 0:
@@ -162,6 +184,28 @@
 
         normalize(1, c)
 
+        if c == 0:
+
+            @pl.when(prompt)
+            def _():
+                pl.semaphore_wait(ack.at[0], 1)
+
+            @pl.when(third_now)
+            def _():
+                pl.semaphore_wait(ack.at[2], 1)
+
+        @pl.when(prompt & on_first)
+        def _():
+            s2(c).start()
+
+        @pl.when(on_second & is_outer)
+        def _():
+            s0(c).start()
+
+        @pl.when(third_now)
+        def _():
+            s5(c).start()
+
     @pl.when(on_second & is_inner)
     def _():
         start(s5)
@@ -176,22 +220,17 @@
     def _():
         start(s0)
 
-    pl.semaphore_wait(ack.at[0], 1)
-
-    @pl.when(on_first)
+    @pl.when(jnp.logical_not(prompt))
+    def _():
+        pl.semaphore_wait(ack.at[0], 1)
+
+    @pl.when(jnp.logical_not(prompt) & on_first)
     def _():
         start(s2)
 
-    @pl.when((on_first & is_inner & jnp.logical_not(ahead_first)) | on_second)
+    @pl.when(is_inner & jnp.logical_not(ahead_first))
     def _():
         start(s0)
-
-    third_now = is_inner & on_first & (along == 1)
-
-    @pl.when(third_now)
-    def _():
-        pl.semaphore_wait(ack.at[2], 1)
-        start(s5)
 
     scale, bias = scaling_in[:1, :1], shift_in[:1, :1]
 
@@ -252,13 +291,19 @@
             def _():
                 s5(c).start()
 
-        far = buf.at[kind, distance, pl.ds(first * R, count * R)]
-        dots = lax.dot_general(buf[other, 0], far[...], (((1,), (1,)), ((), ())), preferred_element_type=jnp.float32)
+        accumulate(kind, buf.at[kind, distance, pl.ds(first * R, count * R)])
+
+    def accumulate(kind, far):
+        other = 1 - kind
+        rows = math.prod(far.shape) // D
+        dots = products(buf.at[other, 0], far, D if rows == WIDE else HALF)
         term, coef = entries(dots, scale, bias)
         loss[kind] += lanes(term)
         for n in range(0, D, 384):
             cols = pl.ds(n, 384)
-            grad[other, :, cols] += jnp.dot(coef, far[:, cols], preferred_element_type=jnp.float32)
+            grad[other, :, cols] += jnp.dot(
+                coef, far[..., cols].reshape(-1, 384), preferred_element_type=jnp.float32
+            )
 
     for half in (0, 1):
         code = outer * OUTER[half] + (1 - outer) * (along * ALONG[half] + (1 - along) * ACROSS[half])
@@ -270,11 +315,19 @@
             if half == 0:
                 pl.when(i == 2)(late_sends)
 
-            @pl.when(item < LATE)
+            @pl.when((item > NOTHING) & (item < LATE))
             def _():
                 use(item, 0, WIDE // R)
 
-            @pl.when(item >= LATE)
+            if half == 1:
+
+                @pl.when(item == BOTH)
+                def _():
+                    arrived(p, 2, NC - 1)
+                    arrived(p, 3, NC - 1)
+                    accumulate(p, buf.at[p, pl.ds(2, 2), pl.ds(WIDE, ROWS - WIDE)])
+
+            @pl.when(item > LATE)
             def _():
                 use(item - LATE, WIDE // R, NC - WIDE // R)
 

time: 53 us -> 53 us (level)
  the two profiles are of different devices: /device:TPU:449 before, /device:TPU:705 now
where the time goes in v5:
time: 53 us; the launch traced here: 52.8 us
  Pallas kernels  50.9 us (96%)
  between operations  1.95 us (4%)
    pallas_call x1, Pallas kernels, local(): pl.pallas_call(functools.partial(kernel, total), out_shape=(jax.ShapeDtyp...  49.1 us
    pallas_call x1, Pallas kernels, local(): pl.pallas_call(hand_over, out_shape=(jax.ShapeDtypeStruct((ROWS,), jnp.fl...  1.78 us

profile of v5, /device:TPU:705, one launch (start us, length us, event | category | flops | bytes accessed | tf_op | source)
XLA Modules:
  0.0 52.8 jit_solution(5737598465717730147)
XLA Ops:
  1.9 49.1 %shard_map.67 = (f32[1,384]{1,0:T(1,128)S(1)}, bf16[384,1152]{1,0:T(8,128)(2,1)S(1)}, bf16[384,1152]{1,0:T(8,128)(2,1)S(1)}) custom-call(f32[8,128]{1,0:T(8,128)S(1)} %broadcast_in_dim.6.scaling_in, f32[8,128]{1,0:T(8,128)S(1)} %broadcast_in_dim.7.shift_in, bf16[384,1152]{1,0:T(8,128)(2,1)} %picture.1, bf16[384,1152]{1,0:T(8,128)(2,1)} %caption.1), custom_call_target="tpu_custom_call" | custom-call | tf_op jit(solution)/shard_map/pallas_call | solution.py:371
  51.0 1.8 %hand_over.1 = (f32[384]{0:T(512)}, bf16[384,1152]{1,0:T(8,128)(2,1)}, bf16[384,1152]{1,0:T(8,128)(2,1)}) custom-call(f32[1,384]{1,0:T(1,128)S(1)} %get-tuple-element.6.loss, bf16[384,1152]{1,0:T(8,128)(2,1)S(1)} %get-tuple-element.7.image, bf16[384,1152]{1,0:T(8,128)(2,1)S(1)} %get-tuple-element.8.text), custom_call_target="tpu_custom_call" | custom-call | tf_op jit(solution)/shard_map/hand_over/pallas_call | solution.py:394
  (2 shorter events, 0.0 us)
